TPU v7x, 32 devices: a whole 2x2x4 slice. The times are simulated.
32 devices in a mesh: die: 2 (over y), row: 4 (over z), col: 4 (over x, core).
Axes of the slice: x: 2, y: 2, z: 4, core: 2. Of those that a mesh axis runs over, the one named last changes fastest.
Arguments:
- parcel_patch: float32 [4, 2048, 256], P('die', ('row', 'col')), may hold values from 0.1 to 1
- target_unit: int32 [4, 2048, 1], P('die', ('row', 'col')), may hold values from 0 to 15; in each aligned block of 128 rows (0 to 127, 128 to 255, ..., all dimensions but the last counted through in order) at most 16 rows name the same one
- target_patch: int32 [4, 2048], P('die', ('row', 'col')), may hold values from 0 to 127
- across_taps: float32 [8, 255], replicated, may hold values from -0.375 to 0.375
- down_taps: float32 [8, 255], replicated, may hold values from -0.375 to 0.375
- source_heated_mixing: float32 [8, 4, 4], replicated, may hold values from -2.4 to 2.4
Outputs:
- chip_heat_increase: float32 [4, 512, 1024], P('die', 'row', 'col')
- block_power_slopes: float32 [4, 2048, 256], P('die', ('row', 'col'))
Inputs may be any that keep to these rules, and one draw needn't show every extreme that they name: `target_unit`: among the 128 blocks of one die held by one device (aligned blocks of rows), at most 16 name the same device, and in every draw some such group names one device exactly 16 times.
All inputs are finite; a program needn't handle non-finite values.
Results may differ from a plain program's by a relative error of at most 0.0002.
Values sent between devices are 32-bit elements; how exact they have to be, the bound alone decides.
A program may use at most 192 MiB of HBM per device.

v0:
```python
import functools

import jax
import jax.numpy as jnp
from jax import lax
from jax.experimental import pallas as pl
from jax.experimental.pallas import tpu as pltpu
from jax.sharding import PartitionSpec as P

PATCH_SIDE = 16
UNIT_MESH_X = 128
UNIT_MESH_Y = 256
HALO = 128


high = lax.Precision.HIGH


def two_halves(values):
    head = values.astype(jnp.bfloat16)
    return head, (values - head.astype(jnp.float32)).astype(jnp.bfloat16)


def stage_kernel(
    is_seed, x_ref, across_ref, down_ref, mix_ref, out_ref,
    pad, a_cat, d_cat, p_cat, y_all, acc, got, send, recv,
):
    here, a, b = x_ref.shape
    terms = across_ref.shape[0]
    h = HALO
    row, col, die = lax.axis_index("row"), lax.axis_index("col"), lax.axis_index("die")
    has_up, has_down = row > 0, row < lax.axis_size("row") - 1
    has_left, has_right = col > 0, col < lax.axis_size("col") - 1
    up, down, left, right = {"row": row - 1}, {"row": row + 1}, {"col": col - 1}, {"col": col + 1}
    other = {"die": 1 - die}
    near = ((has_up, up), (has_down, down), (has_left, left), (has_right, right))

    pad[...] = jnp.zeros_like(pad)
    own = x_ref[...]
    pad[:, h : h + a, h : h + b] = jax.nn.sigmoid(own) if is_seed else own

    barrier = pltpu.get_barrier_semaphore()
    for there, device in near:
        @pl.when(there)
        def _(device=device):
            pl.semaphore_signal(barrier, inc=1, device_id=device, device_id_type=pl.DeviceIdType.MESH)
    pl.semaphore_signal(barrier, inc=1, device_id=other, device_id_type=pl.DeviceIdType.MESH)
    count = jnp.int32(1)
    for there, _ in near:
        count = count + there.astype(jnp.int32)
    pl.semaphore_wait(barrier, count)

    def copy(number, src, dst, device):
        return pltpu.make_async_remote_copy(
            src_ref=src, dst_ref=dst, send_sem=send.at[number], recv_sem=recv.at[number],
            device_id=device, device_id_type=pl.DeviceIdType.MESH,
        )

    tops = (0, h, h + a)
    sizes = (h, a, h)

    def block(band, start, width):
        return pad.at[:, pl.ds(tops[band], sizes[band]), pl.ds(start, width)]

    to_up = copy(0, pad.at[:, pl.ds(h, h), pl.ds(h, b)], block(2, h, b), up)
    to_down = copy(1, pad.at[:, pl.ds(a, h), pl.ds(h, b)], block(0, h, b), down)
    to_left = [copy(2 + k, block(k, h, h), block(k, h + b, h), left) for k in range(3)]
    to_right = [copy(5 + k, block(k, b, h), block(k, 0, h), right) for k in range(3)]

    def start(there, c):
        @pl.when(there)
        def _():
            c.start()

    def ended(there, c):
        @pl.when(there)
        def _():
            c.wait_send()

    def arrived(there, c):
        @pl.when(there)
        def _():
            c.wait_recv()

    start(has_up, to_up)
    start(has_down, to_down)
    start(has_left, to_left[1])
    start(has_right, to_right[1])

    def across_bands(t):
        span = jnp.broadcast_to(across_base[t : t + 1, :], (a, a + 2 * h))
        head, rest = two_halves(pltpu.roll(span, 0, 1, stride=1, stride_axis=0))
        lines = pl.ds(t * a, a)
        w = a + 2 * h
        a_cat[lines, 0:w] = head
        a_cat[lines, w : 2 * w] = head
        a_cat[lines, 2 * w : 3 * w] = rest

    def down_bands(t):
        w = b + 2 * h
        span = jnp.broadcast_to(down_base[t : t + 1, :], (h, 3 * h))
        head, rest = two_halves(pltpu.roll(span, 0, 1, stride=1, stride_axis=0))
        for part in range(3):
            piece = rest if part == 1 else head
            for k in range(b // h):
                lo, hi = k * h, k * h + 3 * h
                lines = pl.ds(k * h, h)
                d_cat[t, lines, part * w + lo : part * w + hi] = piece
                if lo:
                    d_cat[t, lines, part * w : part * w + lo] = jnp.zeros((h, lo), jnp.bfloat16)
                if hi < w:
                    d_cat[t, lines, part * w + hi : part * w + w] = jnp.zeros((h, w - hi), jnp.bfloat16)

    def base(taps_ref):
        taps = taps_ref.shape[1]
        k = lax.broadcasted_iota(jnp.int32, (taps, 3 * h), 0)
        u = lax.broadcasted_iota(jnp.int32, (taps, 3 * h), 1)
        pick = (u == (taps - k if is_seed else k + 1)).astype(jnp.float32)
        return jnp.dot(
            taps_ref[...], pick, precision=lax.Precision.HIGHEST, preferred_element_type=jnp.float32
        )

    across_base, down_base = base(across_ref), base(down_ref)
    for t in range(terms):
        across_bands(t)
    arrived(has_down, to_up)
    for c, there in ((to_left[2], has_left), (to_right[2], has_right)):
        start(jnp.logical_and(has_down, there), c)
    arrived(has_up, to_down)
    for c, there in ((to_left[0], has_left), (to_right[0], has_right)):
        start(jnp.logical_and(has_up, there), c)
    w0, w1 = a + 2 * h, b + 2 * h

    def fill(e, source, at, width):
        head, rest = two_halves(pad[e, :, source : source + width])
        cols = slice(e * w1 + at, e * w1 + at + width)
        p_cat[0:w0, cols] = head
        p_cat[w0 : 2 * w0, cols] = rest
        p_cat[2 * w0 : 3 * w0, cols] = head

    def across(at, width):
        cols = slice(at, at + width)
        y_all[:, cols] = jnp.dot(a_cat[...], p_cat[:, cols], preferred_element_type=jnp.float32)

    for e in range(here):
        fill(e, h, 0, b)
        across(e * w1, b)
    for t in range(terms):
        down_bands(t)
    rows_of = (has_up, None, has_down)
    for k in range(3):
        for there, c in ((has_right, to_left[k]), (has_left, to_right[k])):
            arrived(there if k == 1 else jnp.logical_and(rows_of[k], there), c)
    for e in range(here):
        fill(e, 0, b, h)
        fill(e, h + b, b + h, h)
        across(e * w1 + b, 2 * h)
    acc[...] = jnp.zeros_like(acc)

    def weight(t, d, e):
        mine = die * here + e
        return mix_ref[t, mine * acc.shape[0] + d if is_seed else d * acc.shape[0] + mine]

    def along(t, carry):
        lines = pl.ds(pl.multiple_of(t * a, a), a)
        rows = jnp.concatenate(
            [
                jnp.concatenate(
                    [
                        y_all[lines, e * w1 + b : e * w1 + b + h],
                        y_all[lines, e * w1 : e * w1 + b],
                        y_all[lines, e * w1 + b + h : (e + 1) * w1],
                    ],
                    axis=1,
                )
                for e in range(here)
            ],
            axis=0,
        )
        head, rest = two_halves(rows)
        z = lax.dot_general(
            jnp.concatenate([head, head, rest], axis=1), d_cat[t],
            (((1,), (1,)), ((), ())), preferred_element_type=jnp.float32,
        )
        for d in range(acc.shape[0]):
            total = acc[d]
            for e in range(here):
                total = total + weight(t, d, e) * z[e * a : (e + 1) * a]
            acc[d] = total
        return carry

    lax.fori_loop(0, terms, along, 0)
    share = copy(8, acc.at[pl.ds((1 - die) * here, here)], got, other)
    share.start()
    for there, c in ((has_up, to_up), (has_down, to_down), (has_left, to_left[1]), (has_right, to_right[1])):
        ended(there, c)
    for k in (0, 2):
        for there, c in ((has_left, to_left[k]), (has_right, to_right[k])):
            ended(jnp.logical_and(rows_of[k], there), c)
    share.wait()
    out_ref[...] = acc[pl.ds(die * here, here)] + got[...]


def stage(fields, across_taps, down_taps, mix, is_seed):
    here, a, b = fields.shape
    terms, dies, _ = mix.shape
    w0, w1 = a + 2 * HALO, b + 2 * HALO
    vmem = pl.BlockSpec(memory_space=pltpu.VMEM)
    return pl.pallas_call(
        functools.partial(stage_kernel, is_seed),
        out_shape=jax.ShapeDtypeStruct(fields.shape, jnp.float32),
        in_specs=[vmem, vmem, vmem, pl.BlockSpec(memory_space=pltpu.SMEM)],
        out_specs=vmem,
        scratch_shapes=[
            pltpu.VMEM((here, w0, w1), jnp.float32),
            pltpu.VMEM((terms * a, 3 * w0), jnp.bfloat16),
            pltpu.VMEM((terms, b, 3 * w1), jnp.bfloat16),
            pltpu.VMEM((3 * w0, here * w1), jnp.bfloat16),
            pltpu.VMEM((terms * a, here * w1), jnp.float32),
            pltpu.VMEM((dies, a, b), jnp.float32),
            pltpu.VMEM((here, a, b), jnp.float32),
            pltpu.SemaphoreType.DMA((9,)),
            pltpu.SemaphoreType.DMA((9,)),
        ],
        compiler_params=pltpu.CompilerParams(
            collective_id=1 if is_seed else 0, has_side_effects=True, vmem_limit_bytes=48 * 2**20
        ),
    )(fields, across_taps, down_taps, mix.reshape(terms, dies * dies))


def swap_kernel(*refs):
    count = (len(refs) - 3) // 2
    sources, landed = refs[:count], refs[count : 2 * count]
    send, recv, keep = refs[2 * count :]
    across = lax.axis_size("col")
    peers = across * lax.axis_size("row")
    me = lax.axis_index("row") * across + lax.axis_index("col")
    barrier = pltpu.get_barrier_semaphore()

    def place(number):
        return {"row": number // across, "col": number % across}

    def greet(i, carry):
        pl.semaphore_signal(
            barrier, inc=1, device_id=place((me + i) % peers), device_id_type=pl.DeviceIdType.MESH
        )
        return carry

    def copies(i):
        to = (me + i) % peers
        return [
            pltpu.make_async_remote_copy(
                src_ref=src.at[:, to], dst_ref=dst.at[:, me],
                send_sem=send.at[k, i], recv_sem=recv.at[k, i],
                device_id=place(to), device_id_type=pl.DeviceIdType.MESH,
            )
            for k, (src, dst) in enumerate(zip(sources, landed))
        ]

    def begin(i, carry):
        for c in copies((i + peers // 2 - 2) % (peers - 1) + 1):
            c.start()
        return carry

    def finish(i, carry):
        for c in copies(i):
            c.wait()
        return carry

    lax.fori_loop(1, peers, greet, 0)
    pl.semaphore_wait(barrier, peers - 1)
    lax.fori_loop(1, peers, begin, 0)
    stay = [
        pltpu.make_async_copy(src.at[:, me], dst.at[:, me], keep.at[k])
        for k, (src, dst) in enumerate(zip(sources, landed))
    ]
    for c in stay:
        c.start()
    for c in stay:
        c.wait()
    lax.fori_loop(1, peers, finish, 0)


def swap(arrays, number):
    count, peers = len(arrays), arrays[0].shape[1]
    vmem = pl.BlockSpec(memory_space=pltpu.VMEM)
    return pl.pallas_call(
        swap_kernel,
        out_shape=[jax.ShapeDtypeStruct(x.shape, x.dtype) for x in arrays],
        in_specs=[vmem] * count,
        out_specs=[vmem] * count,
        scratch_shapes=[
            pltpu.SemaphoreType.DMA((count, peers)),
            pltpu.SemaphoreType.DMA((count, peers)),
            pltpu.SemaphoreType.DMA((count,)),
        ],
        compiler_params=pltpu.CompilerParams(
            collective_id=number, has_side_effects=True, vmem_limit_bytes=24 * 2**20
        ),
    )(*arrays)


def tiles_to_map(patch_totals_acc, tiles_down):
    dies_here, tile_total, cell_count = patch_totals_acc.shape
    mesh_layout = patch_totals_acc.reshape(
        dies_here, tile_total // tiles_down, tiles_down, PATCH_SIDE, PATCH_SIDE
    )
    return mesh_layout.transpose(0, 1, 3, 2, 4).reshape(
        dies_here, tile_total // tiles_down * PATCH_SIDE, tiles_down * PATCH_SIDE
    )


def map_to_tiles(source, tiles_down):
    dies_here, rows_all, cols_all = source.shape
    mesh_layout = source.reshape(
        dies_here, rows_all // PATCH_SIDE, PATCH_SIDE, tiles_down, PATCH_SIDE
    )
    return mesh_layout.transpose(0, 1, 3, 2, 4).reshape(dies_here, -1, PATCH_SIDE * PATCH_SIDE)


def local(parcel_patch, target_unit, target_patch, across_taps, down_taps, source_heated_mixing):
    dies_here, blocks_here, cells_tile = parcel_patch.shape
    devices_grid = lax.axis_size(("row", "col"))
    capacity = max(2, 2 * blocks_here // devices_grid)
    tiles_down = UNIT_MESH_Y // PATCH_SIDE
    destination = target_unit[:, :, 0]
    columns = jnp.arange(devices_grid, dtype=jnp.int32)
    same = destination[:, :, None] == destination[:, None, :]
    lines = jnp.arange(blocks_here, dtype=jnp.int32)
    earlier = lines[None, :] < lines[:, None]
    position = jnp.sum((same & earlier[None]).astype(jnp.int32), axis=2)
    slot_index = destination * capacity + position
    slots = jnp.arange(devices_grid * capacity, dtype=jnp.int32)
    place = (slot_index[:, :, None] == slots).astype(jnp.float32)
    outgoing = jnp.einsum("kbs,kbc->ksc", place, parcel_patch, precision=high)
    labels = jnp.sum(place * (target_patch.astype(jnp.float32) + 1.0)[:, :, None], axis=1) - 1.0
    span = dies_here * capacity
    rows = labels.reshape(dies_here, devices_grid, capacity).transpose(1, 0, 2).reshape(1, devices_grid, 1, span)
    rows = jnp.pad(rows, ((0, 0), (0, 0), (0, 0), (0, 128 - span)))
    arrived, arrived_rows = swap(
        (outgoing.reshape(dies_here, devices_grid, capacity, cells_tile), rows), 2
    )
    incoming = arrived.reshape(dies_here, -1, cells_tile)
    arrived_tile = arrived_rows[0, :, 0, :span].reshape(devices_grid, dies_here, capacity).transpose(1, 0, 2)
    target = arrived_tile.reshape(dies_here, -1).astype(jnp.int32)
    chosen = (target[:, :, None] == lines).astype(jnp.float32)
    patch_totals_acc = jnp.einsum("kst,ksc->ktc", chosen, incoming, precision=high)
    wattage_field = tiles_to_map(patch_totals_acc, tiles_down)
    chip_heat_increase = stage(wattage_field, across_taps, down_taps, source_heated_mixing, False)
    adjoint_field_map = stage(chip_heat_increase, across_taps, down_taps, source_heated_mixing, True)
    adjoint_patches = map_to_tiles(adjoint_field_map, tiles_down)
    answers = jnp.einsum("kst,ktc->ksc", chosen, adjoint_patches, precision=high)
    (returned,) = swap((answers.reshape(dies_here, devices_grid, capacity, cells_tile),), 3)
    block_power_slopes = jnp.einsum(
        "kbs,ksc->kbc", place, returned.reshape(dies_here, -1, cells_tile), precision=high
    )
    return (chip_heat_increase, block_power_slopes)


def solution(mesh):
    placed = (
        P("die", ("row", "col"), None),
        P("die", ("row", "col"), None),
        P("die", ("row", "col")),
        P(),
        P(),
        P(),
    )
    return jax.shard_map(
        local,
        mesh=mesh,
        in_specs=placed,
        out_specs=(P("die", "row", "col"), P("die", ("row", "col"), None)),
        check_vma=False,
    )
```

profile of v0, /device:TPU:0, one launch (start us, length us, event | category | flops | bytes accessed | tf_op | source)
XLA Modules:
  0.0 102.2 jit_solution(5120981366917262836)
XLA Ops:
  0.6 0.0 copy-start
  0.6 0.7 convert_add_fusion
  1.4 0.8 copy.28.mix_ref
  2.2 0.9 convert_reduce_fusion
  3.1 0.7 fusion.8
  3.8 0.1 select_reduce_fusion
  3.9 0.1 sub.7
  4.0 0.1 reshape.63
  4.1 0.0 copy-done
  4.1 0.4 fusion.3
  4.6 19.8 %shard_map.77 = (f32[2,16,16,256]{3,2,1,0:T(8,128)S(1)}, f32[1,16,1,128]{3,2,1,0:T(1,128)S(1)}) custom-call(f32[2,16,16,256]{3,2,1,0:T(8,128)S(1)} %bitcast.29, f32[1,16,1,128]{3,2,1,0:T(1,128)S(1)} %pad.4.refs_1_), custom_call_target="tpu_custom_call" | custom-call | tf_op jit(solution)/shard_map/pallas_call | solution.py:287
  24.4 0.1 convert_element_type.29
  24.5 0.1 convert_element_type.31
  24.5 0.5 fusion.1
  25.0 0.6 reshape.65
  25.7 2.0 %copy.35 = f32[2,8,16,16,16]{4,2,3,1,0:T(8,128)} copy(f32[2,8,16,16,16]{4,3,2,1,0:T(8,128)S(1)} %reshape.65) | data formatting | bytes 524288 | tf_op jit(solution)/shard_map/reshape | solution.py:305
  27.7 0.0 copy-start.1
  27.7 0.0 copy-start.2
  27.7 2.5 %reshape.66.x_ref = f32[2,128,256]{2,1,0:T(8,128)S(1)} reshape(f32[2,8,16,16,16]{4,3,2,1,0:T(8,128)} %bitcast.33) | data formatting | bytes 524288 | tf_op jit(solution)/shard_map/reshape | solution.py:308
  30.2 0.0 copy-done.1
  30.2 0.0 copy-done.2
  30.2 23.3 %shard_map.78.x_ref = f32[2,128,256]{2,1,0:T(8,128)S(1)} custom-call(f32[2,128,256]{2,1,0:T(8,128)S(1)} %reshape.66.x_ref, f32[8,255]{1,0:T(8,128)S(1)} %copy-done.1, f32[8,255]{1,0:T(8,128)S(1)} %copy-done.2, f32[8,16]{1,0:T(8,128)S(1)} %copy.28.mix_ref), custom_call_target="tpu_custom_call" | custom-call | tf_op jit(solution)/shard_map/pallas_call | solution.py:209
  53.5 24.2 %shard_map.79 = f32[2,128,256]{2,1,0:T(8,128)S(1)} custom-call(f32[2,128,256]{2,1,0:T(8,128)S(1)} %shard_map.78.x_ref, f32[8,255]{1,0:T(8,128)S(1)} %copy-done.1, f32[8,255]{1,0:T(8,128)S(1)} %copy-done.2, f32[8,16]{1,0:T(8,128)S(1)} %copy.28.mix_ref), custom_call_target="tpu_custom_call" | custom-call | tf_op jit(solution)/shard_map/pallas_call | solution.py:209
  77.6 0.6 reshape.68
  78.3 2.0 %copy.30 = f32[2,8,16,16,16]{4,3,2,1,0:T(8,128)} copy(f32[2,8,16,16,16]{4,2,3,1,0:T(8,128)S(1)} %bitcast.34) | data formatting | bytes 524288 | tf_op jit(solution)/shard_map/transpose | solution.py:318
  80.3 2.4 %reshape.69 = f32[2,128,256]{2,1,0:T(8,128)S(1)} reshape(f32[2,8,16,16,16]{4,3,2,1,0:T(8,128)} %copy.30) | data formatting | bytes 524288 | tf_op jit(solution)/shard_map/reshape | solution.py:318
  82.8 0.4 fusion
  83.1 17.4 %shard_map.80 = f32[2,16,16,256]{3,2,1,0:T(8,128)S(1)} custom-call(f32[2,16,16,256]{3,2,1,0:T(8,128)S(1)} %bitcast.30), custom_call_target="tpu_custom_call" | custom-call | tf_op jit(solution)/shard_map/pallas_call | solution.py:287
  100.5 1.0 fusion.2
  101.5 0.7 copy.38
  (6 shorter events, 0.1 us)
Async XLA Ops:
  0.6 3.5 %copy-start = (f32[2,128,256]{2,1,0:T(8,128)S(1)}, f32[2,128,256]{2,1,0:T(8,128)}, u32[]{:S(2)}) copy-start(f32[2,128,256]{2,1,0:T(8,128)} %param.6) | copy-start | bytes 786436
  27.7 2.5 %copy-start.1 = (f32[8,255]{1,0:T(8,128)S(1)}, f32[8,255]{1,0:T(8,128)}, u32[]{:S(2)}) copy-start(f32[8,255]{1,0:T(8,128)} %across_ref.3) | copy-start | bytes 24484
  27.7 2.5 %copy-start.2 = (f32[8,255]{1,0:T(8,128)S(1)}, f32[8,255]{1,0:T(8,128)}, u32[]{:S(2)}) copy-start(f32[8,255]{1,0:T(8,128)} %down_ref.3) | copy-start | bytes 24484
where the time goes:
time: 102 us
  Pallas kernels  84.6 us (83%)
  local copies, waits for them, and re-layouts  12.1 us (12%)
  other arithmetic  2.54 us (2%)
  matrix products  2.21 us (2%)
    pallas_call x2, Pallas kernels, stage(): pl.pallas_call(functools.partial(stage_kernel, is_seed), out_shape=jax.Sh...  47.4 us
    pallas_call x2, Pallas kernels, swap(): pl.pallas_call(swap_kernel, out_shape=[jax.ShapeDtypeStruct(x.shape, x.dt...  37.1 us
    reshape x2, local copies, waits for them, and re-layouts, tiles_to_map(): patch_totals_acc.reshape(dies_here, tile_total // tiles_down, tiles_down,...  2.66 us
    reshape x1, local copies, waits for them, and re-layouts, tiles_to_map(): mesh_layout.transpose(0, 1, 3, 2, 4)  2.47 us
    reshape x1, local copies, waits for them, and re-layouts, map_to_tiles(): mesh_layout.transpose(0, 1, 3, 2, 4)  2.44 us

commit v1 on v0

v1 whole, which is shorter than its diff:
```python
import functools

import jax
import jax.numpy as jnp
from jax import lax
from jax.experimental import pallas as pl
from jax.experimental.pallas import tpu as pltpu
from jax.sharding import PartitionSpec as P

PATCH_SIDE = 16
UNIT_MESH_X = 128
UNIT_MESH_Y = 256
HALO = 128
MESH = pl.DeviceIdType.MESH


def two_halves(values):
    head = values.astype(jnp.bfloat16)
    return head, (values - head.astype(jnp.float32)).astype(jnp.bfloat16)


def dot(left, right):
    return jnp.dot(left, right, preferred_element_type=jnp.float32)


def iota(shape, dim):
    return lax.broadcasted_iota(jnp.int32, shape, dim)


def exchange_blocks(x):
    rows = x.shape[0]
    left = x[:, :128].reshape(rows // 16, 2, 8, 128)
    right = x[:, 128:].reshape(rows // 16, 2, 8, 128)
    parts = [[left[:, 0], right[:, 0]], [left[:, 1], right[:, 1]]]
    parts[0][1], parts[1][0] = parts[1][0], parts[0][1]
    line, lane = iota((1, 8, 128), 1), iota((1, 8, 128), 2)

    def inner(v):
        for bit in range(3):
            d, w = 1 << bit, 16 << bit
            low_line, low_lane = (line & d) == 0, (lane & w) == 0
            first = pltpu.roll(pltpu.roll(v, 8 - d, 1), w, 2)
            second = first if bit == 2 else pltpu.roll(pltpu.roll(v, d, 1), 128 - w, 2)
            v = jnp.where(low_line == low_lane, v, jnp.where(low_line, first, second))
        return v

    columns = [
        jnp.stack([inner(parts[0][c]), inner(parts[1][c])], axis=1).reshape(rows, 128)
        for c in range(2)
    ]
    return jnp.concatenate(columns, axis=1)


def kernel(
    patch_ref, unit_ref, tile_ref, across_ref, down_ref, mix_ref, heat_ref, slopes_ref,
    outgoing, arrived, answers, returned, label_out, label_in,
    place_keep, chosen_keep, pads, a_own, a_halo, d_cat, p_own, p_halo, y_own, x_cat,
    acc, got, swap_send, swap_recv, label_send, label_recv, halo_send, halo_recv, die_send, die_recv,
):
    here, blocks, cells = patch_ref.shape
    terms = across_ref.shape[0]
    peers, capacity = outgoing.shape[1], outgoing.shape[2]
    slots = peers * capacity
    a, b, h = UNIT_MESH_X, UNIT_MESH_Y, HALO
    tiles = (a // PATCH_SIDE) * (b // PATCH_SIDE)
    row, col, die = lax.axis_index("row"), lax.axis_index("col"), lax.axis_index("die")
    rows_mesh, cols_mesh = lax.axis_size("row"), lax.axis_size("col")
    me = row * cols_mesh + col
    has_up, has_down = row > 0, row < rows_mesh - 1
    has_left, has_right = col > 0, col < cols_mesh - 1
    up, down, left, right = {"row": row - 1}, {"row": row + 1}, {"col": col - 1}, {"col": col + 1}
    other = {"die": 1 - die}

    def place_of(number):
        return {"row": number // cols_mesh, "col": number % cols_mesh}

    pads[...] = jnp.zeros_like(pads)
    barrier = pltpu.get_barrier_semaphore()

    def greet(i, carry):
        pl.semaphore_signal(barrier, inc=1, device_id=place_of((me + i) % peers), device_id_type=MESH)
        return carry

    lax.fori_loop(1, peers, greet, 0)
    pl.semaphore_signal(barrier, inc=1, device_id=other, device_id_type=MESH)

    eye = iota((blocks, blocks), 0) == iota((blocks, blocks), 1)
    before = (iota((blocks, blocks), 1) < iota((blocks, blocks), 0)).astype(jnp.bfloat16)
    lanes = iota((blocks, blocks), 1).astype(jnp.float32)
    slot_lane = iota((blocks, slots), 1).astype(jnp.float32)
    slot_line = iota((slots, blocks), 0).astype(jnp.float32)
    labels, outs = [], []
    for k in range(here):
        dest_row = unit_ref[k : k + 1, :].astype(jnp.float32)
        dest = jnp.sum(jnp.where(eye, dest_row, 0.0), axis=1, keepdims=True)
        named = (dest == lanes).astype(jnp.bfloat16)
        count = dot(before, named)
        position = jnp.sum(named.astype(jnp.float32) * count, axis=1, keepdims=True)
        slot = dest * capacity + position
        place = (slot == slot_lane).astype(jnp.bfloat16)
        place_keep[k] = place
        slot_row = jnp.sum(jnp.where(eye, slot, 0.0), axis=0, keepdims=True)
        place_t = (slot_line == slot_row).astype(jnp.bfloat16)
        head, rest = two_halves(patch_ref[k])
        out = dot(
            jnp.concatenate([place_t, place_t], axis=1), jnp.concatenate([head, rest], axis=0)
        )
        for p in range(peers):
            outgoing[k, p] = out[p * capacity : (p + 1) * capacity]
        tile_row = (tile_ref[k : k + 1, :] + 1).astype(jnp.float32)
        tile_rows = jnp.broadcast_to(tile_row, (16, blocks)).astype(jnp.bfloat16)
        labels.append(dot(tile_rows, place)[0:1])

    slot_row_lane = iota((1, slots), 1)
    mine = jnp.logical_and(slot_row_lane >= me * capacity, slot_row_lane < (me + 1) * capacity)

    def label_rows(p, carry):
        shift = lax.rem((me - p + peers) * capacity, slots)
        rows = [jnp.where(mine, pltpu.roll(x, shift, 1), 0.0) for x in labels]
        label_out[p] = jnp.concatenate(rows, axis=1)
        return carry

    lax.fori_loop(0, peers, label_rows, 0)
    pl.semaphore_wait(barrier, peers)

    def swap_copy(stage, k, i):
        to = (me + i) % peers
        src, dst = (outgoing, arrived) if stage == 0 else (answers, returned)
        return pltpu.make_async_remote_copy(
            src_ref=src.at[k, to], dst_ref=dst.at[k, me],
            send_sem=swap_send.at[stage, k, i], recv_sem=swap_recv.at[stage, k, i],
            device_id=place_of(to), device_id_type=MESH,
        )

    def label_copy(i):
        to = (me + i) % peers
        return pltpu.make_async_remote_copy(
            src_ref=label_out.at[to], dst_ref=label_in.at[me],
            send_sem=label_send.at[i], recv_sem=label_recv.at[i],
            device_id=place_of(to), device_id_type=MESH,
        )

    def each(make, act):
        def body(j, carry):
            getattr(make((j + peers // 2 - 2) % (peers - 1) + 1), act)()
            return carry

        lax.fori_loop(1, peers, body, 0)

    def swap_each(stage, k, act):
        each(functools.partial(swap_copy, stage, k), act)

    def flat(ref, k):
        if capacity % 8 == 0:
            return ref[k].reshape(slots, cells)
        return jnp.concatenate([ref[k, p] for p in range(peers)], axis=0)

    each(label_copy, "start")
    for k in range(here):
        swap_each(0, k, "start")
    label_in[me] = label_out[me]
    for k in range(here):
        arrived[k, me] = outgoing[k, me]

    u0, u1 = iota((across_ref.shape[1], 3 * h), 0), iota((across_ref.shape[1], 3 * h), 1)
    taps = across_ref.shape[1]

    def base(taps_ref, flipped):
        pick = (u1 == (taps - u0 if flipped else u0 + 1)).astype(jnp.float32)
        return jnp.dot(
            taps_ref[...], pick, precision=lax.Precision.HIGHEST, preferred_element_type=jnp.float32
        )

    none = jnp.zeros((h, h), jnp.bfloat16)
    for stage in range(2):
        across_base = base(across_ref, stage == 1)
        down_base = base(down_ref, stage == 0)
        for t in range(terms):
            lines = pl.ds(t * a, a)
            span = jnp.broadcast_to(across_base[t : t + 1, :], (a, 3 * h))
            head, rest = two_halves(pltpu.roll(span, 0, 1, stride=1, stride_axis=0))
            for part, piece in enumerate((head, head, rest)):
                a_own[stage, lines, part * a : (part + 1) * a] = piece[:, h : 2 * h]
                a_halo[stage, lines, part * 2 * h : part * 2 * h + h] = piece[:, :h]
                a_halo[stage, lines, part * 2 * h + h : (part + 1) * 2 * h] = piece[:, 2 * h :]
            wide = jnp.broadcast_to(down_base[t : t + 1, :], (3 * h, 3 * h))
            wide = pltpu.roll(wide, h, 1, stride=1, stride_axis=0)[:, :h]
            w = b + 2 * h
            for part, piece in enumerate(two_halves(wide)):
                at = part * w
                d_cat[stage, t, at : at + b, 0:h] = piece[h : 3 * h]
                d_cat[stage, t, at : at + b, h:b] = piece[0:b]
                d_cat[stage, t, at + b : at + b + h, 0:h] = piece[0:h]
                d_cat[stage, t, at + b : at + b + h, h:b] = none
                d_cat[stage, t, at + b + h : at + w, 0:h] = none
                d_cat[stage, t, at + b + h : at + w, h:b] = piece[2 * h :]

    tops, sizes = (0, h, h + a), (h, a, h)

    def halo(stage, k, number):
        def block(band, start, width):
            return pads.at[stage, k, pl.ds(tops[band], sizes[band]), pl.ds(start, width)]

        if number == 0:
            src, dst, device = block(1, h, b), block(2, h, b), up
        elif number == 1:
            src, dst, device = block(1, h, b), block(0, h, b), down
        elif number < 5:
            src, dst, device = block(number - 2, h, h), block(number - 2, h + b, h), left
        else:
            src, dst, device = block(number - 5, b, h), block(number - 5, 0, h), right
        return pltpu.make_async_remote_copy(
            src_ref=src, dst_ref=dst,
            send_sem=halo_send.at[stage, k, number], recv_sem=halo_recv.at[stage, k, number],
            device_id=device, device_id_type=MESH,
        )

    rows_of = (has_up, None, has_down)

    def both(x, y):
        return y if x is None else jnp.logical_and(x, y)

    sends = [has_up, has_down] + [both(r, has_left) for r in rows_of] + [both(r, has_right) for r in rows_of]
    gets = [has_down, has_up] + [both(r, has_right) for r in rows_of] + [both(r, has_left) for r in rows_of]

    def act(stage, k, number, what):
        @pl.when(gets[number] if what == "wait_recv" else sends[number])
        def _():
            getattr(halo(stage, k, number), what)()

    def begin_halo(stage, k, field):
        pads[stage, k, h : h + a, h : h + b] = field
        for number in (0, 1, 3, 6):
            act(stage, k, number, "start")

    def forward(stage, k):
        act(stage, k, 0, "wait_recv")
        for number in (4, 7):
            act(stage, k, number, "start")
        act(stage, k, 1, "wait_recv")
        for number in (2, 5):
            act(stage, k, number, "start")

    def fill(stage, k, band, source, at, width):
        head, rest = two_halves(pads[stage, k, tops[band] : tops[band] + sizes[band], source : source + width])
        cols = slice(at, at + width)
        if band == 1:
            for part, piece in enumerate((head, rest, head)):
                p_own[k, part * a : (part + 1) * a, cols] = piece
        else:
            off = 0 if band == 0 else h
            for part, piece in enumerate((head, rest, head)):
                p_halo[k, part * 2 * h + off : part * 2 * h + off + h, cols] = piece

    def own_rows(stage, k, at):
        cols = slice(at, at + b)
        y_own[k, :, cols] = dot(a_own[stage], p_own[k, :, cols])

    def far_rows(stage, k, at):
        cols = slice(at, at + b)
        total = dot(a_halo[stage], p_halo[k, :, cols]) + y_own[k, :, cols]
        head, rest = two_halves(total)
        x_cat[k, :, cols] = head
        x_cat[k, :, at + b + 2 * h : at + 2 * b + 2 * h] = rest

    def along(stage, k):
        w = b + 2 * h

        def body(t, carry):
            lines = pl.ds(pl.multiple_of(t * a, a), a)
            head, rest = x_cat[k, lines, :w], x_cat[k, lines, w:]
            d_head, d_rest = d_cat[stage, t, :w], d_cat[stage, t, w:]
            z = dot(
                jnp.concatenate([head, head, rest], axis=1),
                jnp.concatenate([d_head, d_rest, d_head], axis=0),
            )
            source = die * here + k
            for d in range(2 * here):
                target = ((1 - die) if d < here else die) * here + d % here
                weight = mix_ref[t, target, source] if stage == 0 else mix_ref[t, source, target]
                acc[stage, d] = acc[stage, d] + weight * z
            return carry

        lax.fori_loop(0, terms, body, 0)

    def share(stage, k):
        return pltpu.make_async_remote_copy(
            src_ref=acc.at[stage, k], dst_ref=got.at[stage, k],
            send_sem=die_send.at[stage, k], recv_sem=die_recv.at[stage, k],
            device_id=other, device_id_type=MESH,
        )

    def run_stage(stage):
        for k in range(here):
            forward(stage, k)
            for band in (0, 2):
                fill(stage, k, band, h, 0, b)
            far_rows(stage, k, 0)
        for k in range(here):
            for number in (3, 6):
                act(stage, k, number, "wait_recv")
            fill(stage, k, 1, 0, b, h)
            fill(stage, k, 1, h + b, b + h, h)
            own_rows(stage, k, b)
            for number in (2, 4, 5, 7):
                act(stage, k, number, "wait_recv")
            for band in (0, 2):
                fill(stage, k, band, 0, b, h)
                fill(stage, k, band, h + b, b + h, h)
            far_rows(stage, k, b)
            along(stage, k)
        for k in range(here):
            share(stage, k).start()

    acc[...] = jnp.zeros_like(acc)
    each(label_copy, "wait_recv")
    label_all = jnp.sum(label_in[...], axis=0)
    tile_line = (iota((tiles, slots), 0) + 1).astype(jnp.float32)
    tile_lane = (iota((slots, tiles), 1) + 1).astype(jnp.float32)
    eye_slots = iota((slots, slots), 0) == iota((slots, slots), 1)
    for k in range(here):
        label = label_all[:, k * slots : (k + 1) * slots]
        chosen_t = (tile_line == label).astype(jnp.bfloat16)
        label_col = jnp.sum(jnp.where(eye_slots, label, 0.0), axis=1, keepdims=True)
        chosen_keep[k] = (tile_lane == label_col).astype(jnp.bfloat16)
        swap_each(0, k, "wait_recv")
        head, rest = two_halves(flat(arrived, k))
        totals = dot(
            jnp.concatenate([chosen_t, chosen_t], axis=1), jnp.concatenate([head, rest], axis=0)
        )
        begin_halo(0, k, exchange_blocks(totals))
        fill(0, k, 1, h, 0, b)
        own_rows(0, k, 0)
    run_stage(0)
    for k in range(here):
        share(0, k).wait_recv()
        heat = acc[0, here + k] + got[0, k]
        heat_ref[k] = heat
        begin_halo(1, k, jax.nn.sigmoid(heat))
        fill(1, k, 1, h, 0, b)
        own_rows(1, k, 0)
    run_stage(1)
    for k in range(here):
        share(1, k).wait_recv()
        patches = exchange_blocks(acc[1, here + k] + got[1, k])
        head, rest = two_halves(patches)
        chosen = chosen_keep[k]
        answer = dot(jnp.concatenate([chosen, chosen], axis=1), jnp.concatenate([head, rest], axis=0))
        for p in range(peers):
            answers[k, p] = answer[p * capacity : (p + 1) * capacity]
        swap_each(1, k, "start")
        returned[k, me] = answers[k, me]
    for stage in range(2):
        for k in range(here):
            for number in range(8):
                act(stage, k, number, "wait_send")
            share(stage, k).wait_send()
    each(label_copy, "wait_send")
    for k in range(here):
        swap_each(0, k, "wait_send")
    for k in range(here):
        swap_each(1, k, "wait_recv")
        head, rest = two_halves(flat(returned, k))
        place = place_keep[k]
        slopes_ref[k] = dot(
            jnp.concatenate([place, place], axis=1), jnp.concatenate([head, rest], axis=0)
        )
    for k in range(here):
        swap_each(1, k, "wait_send")


def local(parcel_patch, target_unit, target_patch, across_taps, down_taps, source_heated_mixing):
    here, blocks, cells = parcel_patch.shape
    terms, dies, _ = source_heated_mixing.shape
    peers = lax.axis_size(("row", "col"))
    capacity = max(2, 2 * blocks // peers)
    slots = peers * capacity
    a, b, h = UNIT_MESH_X, UNIT_MESH_Y, HALO
    w0, w1 = a + 2 * h, b + 2 * h
    vmem = pl.BlockSpec(memory_space=pltpu.VMEM)
    f32, bf16 = jnp.float32, jnp.bfloat16
    swap_buffer = pltpu.VMEM((here, peers, capacity, cells), f32)
    sems = pltpu.SemaphoreType.DMA
    return pl.pallas_call(
        kernel,
        out_shape=(
            jax.ShapeDtypeStruct((here, a, b), f32),
            jax.ShapeDtypeStruct((here, blocks, cells), f32),
        ),
        in_specs=[vmem] * 5 + [pl.BlockSpec(memory_space=pltpu.SMEM)],
        out_specs=(vmem, vmem),
        scratch_shapes=[
            swap_buffer, swap_buffer, swap_buffer, swap_buffer,
            pltpu.VMEM((peers, 1, here * slots), f32),
            pltpu.VMEM((peers, 1, here * slots), f32),
            pltpu.VMEM((here, blocks, slots), bf16),
            pltpu.VMEM((here, slots, (a // PATCH_SIDE) * (b // PATCH_SIDE)), bf16),
            pltpu.VMEM((2, here, w0, w1), f32),
            pltpu.VMEM((2, terms * a, 3 * a), bf16),
            pltpu.VMEM((2, terms * a, 6 * h), bf16),
            pltpu.VMEM((2, terms, 2 * w1, b), bf16),
            pltpu.VMEM((here, 3 * a, w1), bf16),
            pltpu.VMEM((here, 6 * h, w1), bf16),
            pltpu.VMEM((here, terms * a, w1), f32),
            pltpu.VMEM((here, terms * a, 2 * w1), bf16),
            pltpu.VMEM((2, dies, a, b), f32),
            pltpu.VMEM((2, here, a, b), f32),
            sems((2, here, peers)), sems((2, here, peers)),
            sems((peers,)), sems((peers,)),
            sems((2, here, 8)), sems((2, here, 8)),
            sems((2, here)), sems((2, here)),
        ],
        compiler_params=pltpu.CompilerParams(
            collective_id=0, has_side_effects=True, vmem_limit_bytes=56 * 2**20
        ),
    )(
        parcel_patch, target_unit.reshape(here, blocks), target_patch,
        across_taps, down_taps, source_heated_mixing,
    )


def solution(mesh):
    placed = (
        P("die", ("row", "col"), None),
        P("die", ("row", "col"), None),
        P("die", ("row", "col")),
        P(),
        P(),
        P(),
    )
    return jax.shard_map(
        local,
        mesh=mesh,
        in_specs=placed,
        out_specs=(P("die", "row", "col"), P("die", ("row", "col"), None)),
        check_vma=False,
    )
```

time: 102 us -> 83.5 us (0.82)
  local copies, waits for them, and re-layouts: 12.1 us -> 3.81 us
  Pallas kernels: 84.6 us -> 78.7 us
  other arithmetic: 2.54 us -> 0 us
  matrix products: 2.21 us -> 0 us
    reshape x7 -> x0, local copies, waits for them, and re-layouts: 9.05 us -> none  [the longest x2 2.66 us: tiles_to_map(): patch_totals_acc.reshape(dies_here, tile_total // tiles_down, tiles_down,...]
    pallas_call x4 -> x1, Pallas kernels: 84.6 us -> 78.7 us  [local(): pl.pallas_call(kernel, out_shape=(jax.ShapeDtypeStruct((here, a, b), f32)...]
    unnamed x7 -> x5, local copies, waits for them, and re-layouts: 0.72 us -> 3.81 us
    dot_general x4 -> x0, matrix products: 2.21 us -> none  [the longest x1 0.99 us: local(): jnp.einsum('kbs,ksc->kbc', place, returned.reshape(dies_here, -1, cells_t...]
    transpose x2 -> x0, local copies, waits for them, and re-layouts: 2.04 us -> none  [the longest x1 2.02 us: map_to_tiles(): mesh_layout.transpose(0, 1, 3, 2, 4)]
    reduce_sum x2 -> x0, other arithmetic: 1.07 us -> none  [the longest x1 0.93 us: local(): position = jnp.sum((same & earlier[None]).astype(jnp.int32), axis=2)]
where the time goes in v1:
time: 83.5 us; the launch traced here: 83.2 us
  Pallas kernels  78.7 us (94%)
  local copies, waits for them, and re-layouts  3.81 us (5%)
    pallas_call x1, Pallas kernels, local(): pl.pallas_call(kernel, out_shape=(jax.ShapeDtypeStruct((here, a, b), f32)...  78.7 us
    unnamed x5, local copies, waits for them, and re-layouts  3.81 us

profile of v1, /device:TPU:0, one launch (start us, length us, event | category | flops | bytes accessed | tf_op | source)
XLA Modules:
  0.0 83.2 jit_solution(8417686099611163038)
XLA Ops:
  0.6 1.4 %copy.8.mix_ref = f32[8,4,4]{2,1,0:T(4,128)} copy(f32[8,4,4]{0,2,1:T(4,128)} %param.11) | data formatting | bytes 1024 | tf_op args[5]
  2.0 78.7 %shard_map.77 = (f32[2,128,256]{2,1,0:T(8,128)}, f32[2,128,256]{2,1,0:T(8,128)}) custom-call(f32[2,128,256]{2,1,0:T(8,128)} %patch_ref.1, s32[2,128]{1,0:T(2,128)} %bitcast.1, s32[2,128]{1,0:T(2,128)} %tile_ref.1, f32[8,255]{1,0:T(8,128)} %across_ref.1, f32[8,255]{1,0:T(8,128)} %down_ref.1, f32[8,4,4]{2,1,0:T(4,128)} %copy.8.mix_ref), custom_call_target="tpu_custom_call" | custom-call | tf_op jit(solution)/shard_map/pallas_call | solution.py:384
  80.7 0.0 copy-start
  80.7 1.7 %copy.11 = f32[2,128,256]{2,1,0:T(8,128)} copy(f32[2,128,256]{2,1,0:T(8,128)} %get-tuple-element.4) | data formatting | bytes 524288
  82.5 0.0 copy-done
  82.5 0.7 copy.12
Async XLA Ops:
  80.7 1.7 %copy-start = (f32[2,128,256]{2,1,0:T(8,128)S(1)}, f32[2,128,256]{2,1,0:T(8,128)}, u32[]{:S(2)}) copy-start(f32[2,128,256]{2,1,0:T(8,128)} %get-tuple-element.5) | copy-start | bytes 786436

commit v2 on v1

--- a/solution.py
+++ b/solution.py
@@ -74,7 +74,6 @@
     def place_of(number):
         return {"row": number // cols_mesh, "col": number % cols_mesh}
 
-    pads[...] = jnp.zeros_like(pads)
     barrier = pltpu.get_barrier_semaphore()
 
     def greet(i, carry):
@@ -161,6 +160,18 @@
     label_in[me] = label_out[me]
     for k in range(here):
         arrived[k, me] = outgoing[k, me]
+
+    w0, w1 = a + 2 * h, b + 2 * h
+    for there, lines, cols in (
+        (has_up, slice(0, h), slice(0, w1)),
+        (has_down, slice(h + a, w0), slice(0, w1)),
+        (has_left, slice(0, w0), slice(0, h)),
+        (has_right, slice(0, w0), slice(h + b, w1)),
+    ):
+        @pl.when(jnp.logical_not(there))
+        def _(lines=lines, cols=cols):
+            part = pads[:, :, lines, cols]
+            pads[:, :, lines, cols] = jnp.zeros_like(part)
 
     u0, u1 = iota((across_ref.shape[1], 3 * h), 0), iota((across_ref.shape[1], 3 * h), 1)
     taps = across_ref.shape[1]
@@ -195,16 +206,17 @@
                 d_cat[stage, t, at + b + h : at + w, 0:h] = none
                 d_cat[stage, t, at + b + h : at + w, h:b] = piece[2 * h :]
 
-    tops, sizes = (0, h, h + a), (h, a, h)
+    tops, sizes, half = (0, h, h + a), (h, a, h), a // 2
 
     def halo(stage, k, number):
-        def block(band, start, width):
-            return pads.at[stage, k, pl.ds(tops[band], sizes[band]), pl.ds(start, width)]
-
-        if number == 0:
-            src, dst, device = block(1, h, b), block(2, h, b), up
-        elif number == 1:
-            src, dst, device = block(1, h, b), block(0, h, b), down
+        def block(band, start, width, part=None):
+            lines = pl.ds(tops[band], sizes[band]) if part is None else pl.ds(tops[band] + part * half, half)
+            return pads.at[stage, k, lines, pl.ds(start, width)]
+
+        if number in (0, 8):
+            src, dst, device = block(1, h, b, number // 8), block(2, h, b, number // 8), up
+        elif number in (1, 9):
+            src, dst, device = block(1, h, b, number // 8), block(0, h, b, number // 8), down
         elif number < 5:
             src, dst, device = block(number - 2, h, h), block(number - 2, h + b, h), left
         else:
@@ -221,25 +233,26 @@
         return y if x is None else jnp.logical_and(x, y)
 
     sends = [has_up, has_down] + [both(r, has_left) for r in rows_of] + [both(r, has_right) for r in rows_of]
+    sends = sends + sends[:2]
     gets = [has_down, has_up] + [both(r, has_right) for r in rows_of] + [both(r, has_left) for r in rows_of]
+    gets = gets + gets[:2]
 
     def act(stage, k, number, what):
         @pl.when(gets[number] if what == "wait_recv" else sends[number])
         def _():
             getattr(halo(stage, k, number), what)()
 
-    def begin_halo(stage, k, field):
-        pads[stage, k, h : h + a, h : h + b] = field
-        for number in (0, 1, 3, 6):
+    def begin_halo(stage, k, field, part):
+        pads[stage, k, h + part * half : h + (part + 1) * half, h : h + b] = field
+        for number in (8 * part, 8 * part + 1) + ((3, 6) if part == 1 else ()):
             act(stage, k, number, "start")
 
     def forward(stage, k):
-        act(stage, k, 0, "wait_recv")
-        for number in (4, 7):
-            act(stage, k, number, "start")
-        act(stage, k, 1, "wait_recv")
-        for number in (2, 5):
-            act(stage, k, number, "start")
+        for from_down, corners in ((0, (4, 7)), (1, (2, 5))):
+            for part in range(2):
+                act(stage, k, from_down + 8 * part, "wait_recv")
+            for number in corners:
+                act(stage, k, number, "start")
 
     def fill(stage, k, band, source, at, width):
         head, rest = two_halves(pads[stage, k, tops[band] : tops[band] + sizes[band], source : source + width])
@@ -263,10 +276,11 @@
         x_cat[k, :, cols] = head
         x_cat[k, :, at + b + 2 * h : at + 2 * b + 2 * h] = rest
 
-    def along(stage, k):
+    def along(stage, k, first, last):
         w = b + 2 * h
-
-        def body(t, carry):
+        source = die * here + k
+
+        def body(t, fresh):
             lines = pl.ds(pl.multiple_of(t * a, a), a)
             head, rest = x_cat[k, lines, :w], x_cat[k, lines, w:]
             d_head, d_rest = d_cat[stage, t, :w], d_cat[stage, t, w:]
@@ -274,45 +288,70 @@
                 jnp.concatenate([head, head, rest], axis=1),
                 jnp.concatenate([d_head, d_rest, d_head], axis=0),
             )
-            source = die * here + k
             for d in range(2 * here):
                 target = ((1 - die) if d < here else die) * here + d % here
-                weight = mix_ref[t, target, source] if stage == 0 else mix_ref[t, source, target]
-                acc[stage, d] = acc[stage, d] + weight * z
+                weight = mix_ref[target, source, t] if stage == 0 else mix_ref[source, target, t]
+                acc[stage, d] = weight * z if fresh else acc[stage, d] + weight * z
+
+        if k == 0 and first == 0:
+            body(0, True)
+            first = 1
+
+        def step(t, carry):
+            body(t, False)
             return carry
 
-        lax.fori_loop(0, terms, body, 0)
-
-    def share(stage, k):
+        lax.fori_loop(first, last, step, 0, unroll=True)
+
+    def share(stage, k, part):
+        lines = pl.ds(part * half, half)
         return pltpu.make_async_remote_copy(
-            src_ref=acc.at[stage, k], dst_ref=got.at[stage, k],
-            send_sem=die_send.at[stage, k], recv_sem=die_recv.at[stage, k],
+            src_ref=acc.at[stage, k, lines], dst_ref=got.at[stage, k, lines],
+            send_sem=die_send.at[stage, k, part], recv_sem=die_recv.at[stage, k, part],
             device_id=other, device_id_type=MESH,
         )
 
+    def far_middle(stage, k):
+        for band in (0, 2):
+            fill(stage, k, band, h, 0, b)
+        far_rows(stage, k, 0)
+
+    def own_sides(stage, k):
+        for number in (3, 6):
+            act(stage, k, number, "wait_recv")
+        fill(stage, k, 1, 0, b, h)
+        fill(stage, k, 1, h + b, b + h, h)
+        own_rows(stage, k, b)
+
+    def far_sides(stage, k):
+        for number in (2, 4, 5, 7):
+            act(stage, k, number, "wait_recv")
+        for band in (0, 2):
+            fill(stage, k, band, 0, b, h)
+            fill(stage, k, band, h + b, b + h, h)
+        far_rows(stage, k, b)
+
     def run_stage(stage):
+        last = here - 1
+        for k in range(last):
+            own_sides(stage, k)
+            forward(stage, k)
+            far_middle(stage, k)
+            far_sides(stage, k)
+            if k == last - 1:
+                along(stage, k, 0, terms // 2)
+                own_sides(stage, last)
+                forward(stage, last)
+                along(stage, k, terms // 2, terms)
+            else:
+                along(stage, k, 0, terms)
+        far_middle(stage, last)
+        far_sides(stage, last)
+        along(stage, last, 0, terms)
         for k in range(here):
-            forward(stage, k)
-            for band in (0, 2):
-                fill(stage, k, band, h, 0, b)
-            far_rows(stage, k, 0)
-        for k in range(here):
-            for number in (3, 6):
-                act(stage, k, number, "wait_recv")
-            fill(stage, k, 1, 0, b, h)
-            fill(stage, k, 1, h + b, b + h, h)
-            own_rows(stage, k, b)
-            for number in (2, 4, 5, 7):
-                act(stage, k, number, "wait_recv")
-            for band in (0, 2):
-                fill(stage, k, band, 0, b, h)
-                fill(stage, k, band, h + b, b + h, h)
-            far_rows(stage, k, b)
-            along(stage, k)
-        for k in range(here):
-            share(stage, k).start()
-
-    acc[...] = jnp.zeros_like(acc)
+            for part in range(2):
+                share(stage, k, part).start()
+
     each(label_copy, "wait_recv")
     label_all = jnp.sum(label_in[...], axis=0)
     tile_line = (iota((tiles, slots), 0) + 1).astype(jnp.float32)
@@ -328,20 +367,25 @@
         totals = dot(
             jnp.concatenate([chosen_t, chosen_t], axis=1), jnp.concatenate([head, rest], axis=0)
         )
-        begin_halo(0, k, exchange_blocks(totals))
+        field = exchange_blocks(totals)
+        for part in range(2):
+            begin_halo(0, k, field[part * half : (part + 1) * half], part)
         fill(0, k, 1, h, 0, b)
         own_rows(0, k, 0)
     run_stage(0)
     for k in range(here):
-        share(0, k).wait_recv()
-        heat = acc[0, here + k] + got[0, k]
-        heat_ref[k] = heat
-        begin_halo(1, k, jax.nn.sigmoid(heat))
+        for part in range(2):
+            share(0, k, part).wait_recv()
+            lines = slice(part * half, (part + 1) * half)
+            heat = acc[0, here + k, lines] + got[0, k, lines]
+            heat_ref[k, lines] = heat
+            begin_halo(1, k, jax.nn.sigmoid(heat), part)
         fill(1, k, 1, h, 0, b)
         own_rows(1, k, 0)
     run_stage(1)
     for k in range(here):
-        share(1, k).wait_recv()
+        for part in range(2):
+            share(1, k, part).wait_recv()
         patches = exchange_blocks(acc[1, here + k] + got[1, k])
         head, rest = two_halves(patches)
         chosen = chosen_keep[k]
@@ -352,9 +396,10 @@
         returned[k, me] = answers[k, me]
     for stage in range(2):
         for k in range(here):
-            for number in range(8):
+            for number in range(10):
                 act(stage, k, number, "wait_send")
-            share(stage, k).wait_send()
+            for part in range(2):
+                share(stage, k, part).wait_send()
     each(label_copy, "wait_send")
     for k in range(here):
         swap_each(0, k, "wait_send")
@@ -407,15 +452,15 @@
             pltpu.VMEM((2, here, a, b), f32),
             sems((2, here, peers)), sems((2, here, peers)),
             sems((peers,)), sems((peers,)),
-            sems((2, here, 8)), sems((2, here, 8)),
-            sems((2, here)), sems((2, here)),
+            sems((2, here, 10)), sems((2, here, 10)),
+            sems((2, here, 2)), sems((2, here, 2)),
         ],
         compiler_params=pltpu.CompilerParams(
             collective_id=0, has_side_effects=True, vmem_limit_bytes=56 * 2**20
         ),
     )(
         parcel_patch, target_unit.reshape(here, blocks), target_patch,
-        across_taps, down_taps, source_heated_mixing,
+        across_taps, down_taps, source_heated_mixing.transpose(1, 2, 0),
     )
 
 

time: 83.5 us -> 77.4 us (0.927)
  Pallas kernels: 78.7 us -> 74.1 us
  local copies, waits for them, and re-layouts: 3.81 us -> 2.42 us
    pallas_call x1, Pallas kernels: 78.7 us -> 74.1 us  [local(): pl.pallas_call(kernel, out_shape=(jax.ShapeDtypeStruct((here, a, b), f32)...]
    unnamed x5 -> x4, local copies, waits for them, and re-layouts: 3.81 us -> 2.42 us
where the time goes in v2:
time: 77.4 us; the launch traced here: 77.2 us
  Pallas kernels  74.1 us (96%)
  local copies, waits for them, and re-layouts  2.42 us (3%)
    pallas_call x1, Pallas kernels, local(): pl.pallas_call(kernel, out_shape=(jax.ShapeDtypeStruct((here, a, b), f32)...  74.1 us
    unnamed x4, local copies, waits for them, and re-layouts  2.42 us

profile of v2, /device:TPU:0, one launch (start us, length us, event | category | flops | bytes accessed | tf_op | source)
XLA Modules:
  0.0 77.2 jit_solution(3683996480435520186)
XLA Ops:
  0.6 74.1 %shard_map.77 = (f32[2,128,256]{2,1,0:T(8,128)}, f32[2,128,256]{2,1,0:T(8,128)}) custom-call(f32[2,128,256]{2,1,0:T(8,128)} %patch_ref.1, s32[2,128]{1,0:T(2,128)} %bitcast.3, s32[2,128]{1,0:T(2,128)} %tile_ref.1, f32[8,255]{1,0:T(8,128)} %across_ref.1, f32[8,255]{1,0:T(8,128)} %down_ref.1, f32[4,4,8]{2,1,0:T(4,128)} %bitcast.2), custom_call_target="tpu_custom_call" | custom-call | tf_op jit(solution)/shard_map/pallas_call | solution.py:429
  74.8 0.0 copy-start
  74.8 1.7 %copy.10 = f32[2,128,256]{2,1,0:T(8,128)} copy(f32[2,128,256]{2,1,0:T(8,128)} %get-tuple-element.4) | data formatting | bytes 524288
  76.5 0.0 copy-done
  76.5 0.7 copy.11
Async XLA Ops:
  74.8 1.7 %copy-start = (f32[2,128,256]{2,1,0:T(8,128)S(1)}, f32[2,128,256]{2,1,0:T(8,128)}, u32[]{:S(2)}) copy-start(f32[2,128,256]{2,1,0:T(8,128)} %get-tuple-element.5) | copy-start | bytes 786436

commit v3 on v2

--- a/solution.py
+++ b/solution.py
@@ -52,10 +52,11 @@
 
 
 def kernel(
-    patch_ref, unit_ref, tile_ref, across_ref, down_ref, mix_ref, heat_ref, slopes_ref,
-    outgoing, arrived, answers, returned, label_out, label_in,
+    patch_in, unit_in, tile_in, across_in, down_in, mix_ref, heat_out, slopes_out,
+    patch_ref, unit_ref, tile_ref, across_ref, down_ref, heat_ref, slopes_ref, in_sems, out_sems,
+    outgoing, arrived, answers, returned, label_out, label_in, label_rows,
     place_keep, chosen_keep, pads, a_own, a_halo, d_cat, p_own, p_halo, y_own, x_cat,
-    acc, got, swap_send, swap_recv, label_send, label_recv, halo_send, halo_recv, die_send, die_recv,
+    z_all, acc, got, swap_send, swap_recv, label_sems, halo_send, halo_recv, die_send, die_recv,
 ):
     here, blocks, cells = patch_ref.shape
     terms = across_ref.shape[0]
@@ -74,6 +75,15 @@
     def place_of(number):
         return {"row": number // cols_mesh, "col": number % cols_mesh}
 
+    loads = [
+        pltpu.make_async_copy(src, dst, in_sems.at[i])
+        for i, (src, dst) in enumerate((
+            (unit_in, unit_ref), (tile_in, tile_ref), (patch_in, patch_ref),
+            (across_in, across_ref), (down_in, down_ref),
+        ))
+    ]
+    for load in loads:
+        load.start()
     barrier = pltpu.get_barrier_semaphore()
 
     def greet(i, carry):
@@ -83,21 +93,25 @@
     lax.fori_loop(1, peers, greet, 0)
     pl.semaphore_signal(barrier, inc=1, device_id=other, device_id_type=MESH)
 
+    for load in loads[:3]:
+        load.wait()
     eye = iota((blocks, blocks), 0) == iota((blocks, blocks), 1)
     before = (iota((blocks, blocks), 1) < iota((blocks, blocks), 0)).astype(jnp.bfloat16)
-    lanes = iota((blocks, blocks), 1).astype(jnp.float32)
+    lanes = iota((blocks, 128), 1).astype(jnp.float32)
     slot_lane = iota((blocks, slots), 1).astype(jnp.float32)
     slot_line = iota((slots, blocks), 0).astype(jnp.float32)
-    labels, outs = [], []
-    for k in range(here):
+    peer_line = iota((peers, blocks), 0).astype(jnp.float32)
+
+    def column(line):
+        return jnp.sum(jnp.where(eye, line, 0.0), axis=1, keepdims=True)
+
+    def route(k):
         dest_row = unit_ref[k : k + 1, :].astype(jnp.float32)
-        dest = jnp.sum(jnp.where(eye, dest_row, 0.0), axis=1, keepdims=True)
+        dest = column(dest_row)
         named = (dest == lanes).astype(jnp.bfloat16)
         count = dot(before, named)
         position = jnp.sum(named.astype(jnp.float32) * count, axis=1, keepdims=True)
         slot = dest * capacity + position
-        place = (slot == slot_lane).astype(jnp.bfloat16)
-        place_keep[k] = place
         slot_row = jnp.sum(jnp.where(eye, slot, 0.0), axis=0, keepdims=True)
         place_t = (slot_line == slot_row).astype(jnp.bfloat16)
         head, rest = two_halves(patch_ref[k])
@@ -106,59 +120,70 @@
         )
         for p in range(peers):
             outgoing[k, p] = out[p * capacity : (p + 1) * capacity]
-        tile_row = (tile_ref[k : k + 1, :] + 1).astype(jnp.float32)
-        tile_rows = jnp.broadcast_to(tile_row, (16, blocks)).astype(jnp.bfloat16)
-        labels.append(dot(tile_rows, place)[0:1])
-
-    slot_row_lane = iota((1, slots), 1)
-    mine = jnp.logical_and(slot_row_lane >= me * capacity, slot_row_lane < (me + 1) * capacity)
-
-    def label_rows(p, carry):
-        shift = lax.rem((me - p + peers) * capacity, slots)
-        rows = [jnp.where(mine, pltpu.roll(x, shift, 1), 0.0) for x in labels]
-        label_out[p] = jnp.concatenate(rows, axis=1)
-        return carry
-
-    lax.fori_loop(0, peers, label_rows, 0)
-    pl.semaphore_wait(barrier, peers)
+        return dest_row, position, slot
+
+    def label_part(k, dest_row, position):
+        tile = column((tile_ref[k : k + 1, :] + 1).astype(jnp.float32))
+        spread = jnp.where(lanes == position + k * capacity, tile, 0.0).astype(jnp.bfloat16)
+        return dot((peer_line == dest_row).astype(jnp.bfloat16), spread)
 
     def swap_copy(stage, k, i):
         to = (me + i) % peers
         src, dst = (outgoing, arrived) if stage == 0 else (answers, returned)
         return pltpu.make_async_remote_copy(
             src_ref=src.at[k, to], dst_ref=dst.at[k, me],
-            send_sem=swap_send.at[stage, k, i], recv_sem=swap_recv.at[stage, k, i],
+            send_sem=swap_send.at[stage, k], recv_sem=swap_recv.at[stage, k],
             device_id=place_of(to), device_id_type=MESH,
+        )
+
+    def swap_all(stage, k):
+        src, dst = (outgoing, arrived) if stage == 0 else (answers, returned)
+        return pltpu.make_async_remote_copy(
+            src_ref=src.at[k, pl.ds(0, peers - 1)], dst_ref=dst.at[k, pl.ds(0, peers - 1)],
+            send_sem=swap_send.at[stage, k], recv_sem=swap_recv.at[stage, k],
+            device_id=other, device_id_type=MESH,
         )
 
     def label_copy(i):
         to = (me + i) % peers
         return pltpu.make_async_remote_copy(
             src_ref=label_out.at[to], dst_ref=label_in.at[me],
-            send_sem=label_send.at[i], recv_sem=label_recv.at[i],
+            send_sem=label_sems.at[0], recv_sem=label_sems.at[1],
             device_id=place_of(to), device_id_type=MESH,
         )
 
-    def each(make, act):
+    def label_all():
+        return pltpu.make_async_remote_copy(
+            src_ref=label_out.at[pl.ds(0, peers - 1)], dst_ref=label_in.at[pl.ds(0, peers - 1)],
+            send_sem=label_sems.at[0], recv_sem=label_sems.at[1],
+            device_id=other, device_id_type=MESH,
+        )
+
+    def start_each(make):
         def body(j, carry):
-            getattr(make((j + peers // 2 - 2) % (peers - 1) + 1), act)()
+            make((j + peers // 2 - 2) % (peers - 1) + 1).start()
             return carry
 
         lax.fori_loop(1, peers, body, 0)
-
-    def swap_each(stage, k, act):
-        each(functools.partial(swap_copy, stage, k), act)
 
     def flat(ref, k):
         if capacity % 8 == 0:
             return ref[k].reshape(slots, cells)
         return jnp.concatenate([ref[k, p] for p in range(peers)], axis=0)
 
-    each(label_copy, "start")
-    for k in range(here):
-        swap_each(0, k, "start")
+    routes = [route(0)]
+    pl.semaphore_wait(barrier, peers)
+    start_each(functools.partial(swap_copy, 0, 0))
+    routes += [route(k) for k in range(1, here)]
+    label_sum = sum(label_part(k, *routes[k][:2]) for k in range(here))
+    for p in range(peers):
+        label_out[p] = label_sum[p : p + 1]
+    start_each(label_copy)
+    for k in range(1, here):
+        start_each(functools.partial(swap_copy, 0, k))
     label_in[me] = label_out[me]
     for k in range(here):
+        place_keep[k] = (routes[k][2] == slot_lane).astype(jnp.bfloat16)
         arrived[k, me] = outgoing[k, me]
 
     w0, w1 = a + 2 * h, b + 2 * h
@@ -173,6 +198,8 @@
             part = pads[:, :, lines, cols]
             pads[:, :, lines, cols] = jnp.zeros_like(part)
 
+    for load in loads[3:]:
+        load.wait()
     u0, u1 = iota((across_ref.shape[1], 3 * h), 0), iota((across_ref.shape[1], 3 * h), 1)
     taps = across_ref.shape[1]
 
@@ -276,32 +303,42 @@
         x_cat[k, :, cols] = head
         x_cat[k, :, at + b + 2 * h : at + 2 * b + 2 * h] = rest
 
-    def along(stage, k, first, last):
+    def along(stage, k, at):
         w = b + 2 * h
-        source = die * here + k
-
-        def body(t, fresh):
+        head_cols, rest_cols = slice(at, at + b), slice(w + at, w + at + b)
+
+        def step(t, carry):
             lines = pl.ds(pl.multiple_of(t * a, a), a)
-            head, rest = x_cat[k, lines, :w], x_cat[k, lines, w:]
-            d_head, d_rest = d_cat[stage, t, :w], d_cat[stage, t, w:]
+            head, rest = x_cat[k, lines, head_cols], x_cat[k, lines, rest_cols]
+            d_head, d_rest = d_cat[stage, t, head_cols], d_cat[stage, t, rest_cols]
             z = dot(
                 jnp.concatenate([head, head, rest], axis=1),
                 jnp.concatenate([d_head, d_rest, d_head], axis=0),
             )
-            for d in range(2 * here):
-                target = ((1 - die) if d < here else die) * here + d % here
-                weight = mix_ref[target, source, t] if stage == 0 else mix_ref[source, target, t]
-                acc[stage, d] = weight * z if fresh else acc[stage, d] + weight * z
-
-        if k == 0 and first == 0:
-            body(0, True)
-            first = 1
-
-        def step(t, carry):
-            body(t, False)
+            z_all[k, t] = z if at == 0 else z_all[k, t] + z
             return carry
 
-        lax.fori_loop(first, last, step, 0, unroll=True)
+        lax.fori_loop(0, terms, step, 0, unroll=True)
+
+    def mix(stage, d, part):
+        target = ((1 - die) if d < here else die) * here + d % here
+        weights = []
+        for k in range(here):
+            source = die * here + k
+            for t in range(terms):
+                pair = (target, source) if stage == 0 else (source, target)
+                weights.append(mix_ref[pair[0], pair[1], t])
+
+        def step(i, carry):
+            lines = pl.ds(pl.multiple_of(part * half + i * 16, 16), 16)
+            total = jnp.zeros((16, b), jnp.float32)
+            for k in range(here):
+                for t in range(terms):
+                    total = total + weights[k * terms + t] * z_all[k, t, lines]
+            acc[stage, d, lines] = total
+            return carry
+
+        lax.fori_loop(0, half // 16, step, 0)
 
     def share(stage, k, part):
         lines = pl.ds(part * half, half)
@@ -332,37 +369,41 @@
         far_rows(stage, k, b)
 
     def run_stage(stage):
-        last = here - 1
-        for k in range(last):
-            own_sides(stage, k)
-            forward(stage, k)
+        own_sides(stage, 0)
+        for k in range(here):
+            if k == 0:
+                forward(stage, k)
             far_middle(stage, k)
+            along(stage, k, 0)
             far_sides(stage, k)
-            if k == last - 1:
-                along(stage, k, 0, terms // 2)
-                own_sides(stage, last)
-                forward(stage, last)
-                along(stage, k, terms // 2, terms)
-            else:
-                along(stage, k, 0, terms)
-        far_middle(stage, last)
-        far_sides(stage, last)
-        along(stage, last, 0, terms)
+            if k + 1 < here:
+                own_sides(stage, k + 1)
+                forward(stage, k + 1)
+            along(stage, k, b)
         for k in range(here):
             for part in range(2):
+                mix(stage, k, part)
                 share(stage, k, part).start()
-
-    each(label_copy, "wait_recv")
-    label_all = jnp.sum(label_in[...], axis=0)
+        for k in range(here):
+            for part in range(2):
+                mix(stage, here + k, part)
+
+    label_all().wait_recv()
+    for p in range(peers):
+        label_rows[p : p + 1] = label_in[p]
+    label_flat = label_rows[...].astype(jnp.bfloat16)
+    lane_of = iota((128, slots), 1) % capacity
+    held = iota((peers, slots), 1) // capacity == iota((peers, slots), 0)
     tile_line = (iota((tiles, slots), 0) + 1).astype(jnp.float32)
     tile_lane = (iota((slots, tiles), 1) + 1).astype(jnp.float32)
     eye_slots = iota((slots, slots), 0) == iota((slots, slots), 1)
     for k in range(here):
-        label = label_all[:, k * slots : (k + 1) * slots]
+        pick = (iota((128, slots), 0) == lane_of + k * capacity).astype(jnp.bfloat16)
+        label = jnp.sum(jnp.where(held, dot(label_flat, pick), 0.0), axis=0, keepdims=True)
         chosen_t = (tile_line == label).astype(jnp.bfloat16)
         label_col = jnp.sum(jnp.where(eye_slots, label, 0.0), axis=1, keepdims=True)
         chosen_keep[k] = (tile_lane == label_col).astype(jnp.bfloat16)
-        swap_each(0, k, "wait_recv")
+        swap_all(0, k).wait_recv()
         head, rest = two_halves(flat(arrived, k))
         totals = dot(
             jnp.concatenate([chosen_t, chosen_t], axis=1), jnp.concatenate([head, rest], axis=0)
@@ -382,6 +423,8 @@
             begin_halo(1, k, jax.nn.sigmoid(heat), part)
         fill(1, k, 1, h, 0, b)
         own_rows(1, k, 0)
+    heat_done = pltpu.make_async_copy(heat_ref, heat_out, out_sems.at[here])
+    heat_done.start()
     run_stage(1)
     for k in range(here):
         for part in range(2):
@@ -392,7 +435,7 @@
         answer = dot(jnp.concatenate([chosen, chosen], axis=1), jnp.concatenate([head, rest], axis=0))
         for p in range(peers):
             answers[k, p] = answer[p * capacity : (p + 1) * capacity]
-        swap_each(1, k, "start")
+        start_each(functools.partial(swap_copy, 1, k))
         returned[k, me] = answers[k, me]
     for stage in range(2):
         for k in range(here):
@@ -400,18 +443,37 @@
                 act(stage, k, number, "wait_send")
             for part in range(2):
                 share(stage, k, part).wait_send()
-    each(label_copy, "wait_send")
-    for k in range(here):
-        swap_each(0, k, "wait_send")
-    for k in range(here):
-        swap_each(1, k, "wait_recv")
+    label_all().wait_send()
+    for k in range(here):
+        swap_all(0, k).wait_send()
+    for k in range(here):
+        swap_all(1, k).wait_recv()
         head, rest = two_halves(flat(returned, k))
         place = place_keep[k]
         slopes_ref[k] = dot(
             jnp.concatenate([place, place], axis=1), jnp.concatenate([head, rest], axis=0)
         )
-    for k in range(here):
-        swap_each(1, k, "wait_send")
+        pltpu.make_async_copy(slopes_ref.at[k], slopes_out.at[k], out_sems.at[k]).start()
+    for k in range(here):
+        swap_all(1, k).wait_send()
+    heat_done.wait()
+    for k in range(here):
+        pltpu.make_async_copy(slopes_ref.at[k], slopes_out.at[k], out_sems.at[k]).wait()
+
+
+def finish_kernel(heat_in, slopes_in, heat_out, slopes_out):
+    heat_out[...] = heat_in[...]
+    slopes_out[...] = slopes_in[...]
+
+
+def finish(heat, slopes):
+    vmem = pl.BlockSpec(memory_space=pltpu.VMEM)
+    return pl.pallas_call(
+        finish_kernel,
+        out_shape=tuple(jax.ShapeDtypeStruct(x.shape, x.dtype) for x in (heat, slopes)),
+        in_specs=[vmem, vmem],
+        out_specs=(vmem, vmem),
+    )(heat, slopes)
 
 
 def local(parcel_patch, target_unit, target_patch, across_taps, down_taps, source_heated_mixing):
@@ -422,22 +484,31 @@
     slots = peers * capacity
     a, b, h = UNIT_MESH_X, UNIT_MESH_Y, HALO
     w0, w1 = a + 2 * h, b + 2 * h
-    vmem = pl.BlockSpec(memory_space=pltpu.VMEM)
+    anywhere = pl.BlockSpec(memory_space=pl.ANY)
     f32, bf16 = jnp.float32, jnp.bfloat16
     swap_buffer = pltpu.VMEM((here, peers, capacity, cells), f32)
     sems = pltpu.SemaphoreType.DMA
-    return pl.pallas_call(
+    heat, slopes = pl.pallas_call(
         kernel,
         out_shape=(
             jax.ShapeDtypeStruct((here, a, b), f32),
             jax.ShapeDtypeStruct((here, blocks, cells), f32),
         ),
-        in_specs=[vmem] * 5 + [pl.BlockSpec(memory_space=pltpu.SMEM)],
-        out_specs=(vmem, vmem),
+        in_specs=[anywhere] * 5 + [pl.BlockSpec(memory_space=pltpu.SMEM)],
+        out_specs=(anywhere, anywhere),
         scratch_shapes=[
+            pltpu.VMEM(parcel_patch.shape, f32),
+            pltpu.VMEM((here, blocks), jnp.int32),
+            pltpu.VMEM((here, blocks), jnp.int32),
+            pltpu.VMEM(across_taps.shape, f32),
+            pltpu.VMEM(down_taps.shape, f32),
+            pltpu.VMEM((here, a, b), f32),
+            pltpu.VMEM((here, blocks, cells), f32),
+            sems((5,)), sems((here + 1,)),
             swap_buffer, swap_buffer, swap_buffer, swap_buffer,
-            pltpu.VMEM((peers, 1, here * slots), f32),
-            pltpu.VMEM((peers, 1, here * slots), f32),
+            pltpu.VMEM((peers, 1, 128), f32),
+            pltpu.VMEM((peers, 1, 128), f32),
+            pltpu.VMEM((peers, 128), f32),
             pltpu.VMEM((here, blocks, slots), bf16),
             pltpu.VMEM((here, slots, (a // PATCH_SIDE) * (b // PATCH_SIDE)), bf16),
             pltpu.VMEM((2, here, w0, w1), f32),
@@ -448,10 +519,10 @@
             pltpu.VMEM((here, 6 * h, w1), bf16),
             pltpu.VMEM((here, terms * a, w1), f32),
             pltpu.VMEM((here, terms * a, 2 * w1), bf16),
+            pltpu.VMEM((here, terms, a, b), f32),
             pltpu.VMEM((2, dies, a, b), f32),
             pltpu.VMEM((2, here, a, b), f32),
-            sems((2, here, peers)), sems((2, here, peers)),
-            sems((peers,)), sems((peers,)),
+            sems((2, here)), sems((2, here)), sems((2,)),
             sems((2, here, 10)), sems((2, here, 10)),
             sems((2, here, 2)), sems((2, here, 2)),
         ],
@@ -462,6 +533,7 @@
         parcel_patch, target_unit.reshape(here, blocks), target_patch,
         across_taps, down_taps, source_heated_mixing.transpose(1, 2, 0),
     )
+    return finish(heat, slopes)
 
 
 def solution(mesh):

time: 77.4 us -> 73.7 us (0.952)
  local copies, waits for them, and re-layouts: 2.42 us -> 0 us
  Pallas kernels: 74.1 us -> 72.8 us
    pallas_call x1, Pallas kernels: 74.1 us -> 71 us  [local(): pl.pallas_call(kernel, out_shape=(jax.ShapeDtypeStruct((here, a, b), f32)...]
    unnamed x4 -> x0, local copies, waits for them, and re-layouts: 2.42 us -> none
    pallas_call x0 -> x1, Pallas kernels: none -> 1.84 us  [finish(): pl.pallas_call(finish_kernel, out_shape=tuple((jax.ShapeDtypeStruct(x.sha...]
where the time goes in v3:
time: 73.7 us; the launch traced here: 73.4 us
  Pallas kernels  72.8 us (99%)
    pallas_call x1, Pallas kernels, local(): pl.pallas_call(kernel, out_shape=(jax.ShapeDtypeStruct((here, a, b), f32)...  71 us
    pallas_call x1, Pallas kernels, finish(): pl.pallas_call(finish_kernel, out_shape=tuple((jax.ShapeDtypeStruct(x.sha...  1.84 us

profile of v3, /device:TPU:0, one launch (start us, length us, event | category | flops | bytes accessed | tf_op | source)
XLA Modules:
  0.0 73.4 jit_solution(11042284784715689938)
XLA Ops:
  0.6 71.0 %shard_map.77 = (f32[2,128,256]{2,1,0:T(8,128)}, f32[2,128,256]{2,1,0:T(8,128)}) custom-call(f32[2,128,256]{2,1,0:T(8,128)} %patch_in.1, s32[2,128]{1,0:T(2,128)} %bitcast.3, s32[2,128]{1,0:T(2,128)} %tile_in.1, f32[8,255]{1,0:T(8,128)} %across_in.1, f32[8,255]{1,0:T(8,128)} %down_in.1, f32[4,4,8]{2,1,0:T(4,128)} %bitcast.2), custom_call_target="tpu_custom_call" | custom-call | tf_op jit(solution)/shard_map/pallas_call | solution.py:491
  71.6 1.8 %shard_map.78 = (f32[2,128,256]{2,1,0:T(8,128)}, f32[2,128,256]{2,1,0:T(8,128)}) custom-call(f32[2,128,256]{2,1,0:T(8,128)} %get-tuple-element.4.heat_in, f32[2,128,256]{2,1,0:T(8,128)} %get-tuple-element.5.slopes_in), custom_call_target="tpu_custom_call" | custom-call | tf_op jit(solution)/shard_map/pallas_call | solution.py:471

commit v4 on v3

--- a/solution.py
+++ b/solution.py
@@ -51,10 +51,17 @@
     return jnp.concatenate(columns, axis=1)
 
 
+def flat(parts):
+    peers, capacity, cells = parts.shape
+    if capacity % 8 == 0:
+        return parts.reshape(peers * capacity, cells)
+    return jnp.concatenate([parts[p] for p in range(peers)], axis=0)
+
+
 def kernel(
-    patch_in, unit_in, tile_in, across_in, down_in, mix_ref, heat_out, slopes_out,
-    patch_ref, unit_ref, tile_ref, across_ref, down_ref, heat_ref, slopes_ref, in_sems, out_sems,
-    outgoing, arrived, answers, returned, label_out, label_in, label_rows,
+    patch_in, unit_in, tile_in, across_in, down_in, mix_ref, heat_out, returned, place_out,
+    patch_ref, unit_ref, tile_ref, across_ref, down_ref, heat_ref, in_sems, out_sems,
+    outgoing, arrived, answers, label_out, label_in, label_rows,
     place_keep, chosen_keep, pads, a_own, a_halo, d_cat, p_own, p_halo, y_own, x_cat,
     z_all, acc, got, swap_send, swap_recv, label_sems, halo_send, halo_recv, die_send, die_recv,
 ):
@@ -166,11 +173,6 @@
 
         lax.fori_loop(1, peers, body, 0)
 
-    def flat(ref, k):
-        if capacity % 8 == 0:
-            return ref[k].reshape(slots, cells)
-        return jnp.concatenate([ref[k, p] for p in range(peers)], axis=0)
-
     routes = [route(0)]
     pl.semaphore_wait(barrier, peers)
     start_each(functools.partial(swap_copy, 0, 0))
@@ -185,6 +187,8 @@
     for k in range(here):
         place_keep[k] = (routes[k][2] == slot_lane).astype(jnp.bfloat16)
         arrived[k, me] = outgoing[k, me]
+    place_done = pltpu.make_async_copy(place_keep, place_out, out_sems.at[0])
+    place_done.start()
 
     w0, w1 = a + 2 * h, b + 2 * h
     for there, lines, cols in (
@@ -235,22 +239,22 @@
 
     tops, sizes, half = (0, h, h + a), (h, a, h), a // 2
 
-    def halo(stage, k, number):
-        def block(band, start, width, part=None):
+    def halo(stage, which, number, part=None):
+        def block(band, start, width):
             lines = pl.ds(tops[band], sizes[band]) if part is None else pl.ds(tops[band] + part * half, half)
-            return pads.at[stage, k, lines, pl.ds(start, width)]
-
-        if number in (0, 8):
-            src, dst, device = block(1, h, b, number // 8), block(2, h, b, number // 8), up
-        elif number in (1, 9):
-            src, dst, device = block(1, h, b, number // 8), block(0, h, b, number // 8), down
+            return pads.at[stage, which, lines, pl.ds(start, width)]
+
+        if number == 0:
+            src, dst, device = block(1, h, b), block(2, h, b), up
+        elif number == 1:
+            src, dst, device = block(1, h, b), block(0, h, b), down
         elif number < 5:
             src, dst, device = block(number - 2, h, h), block(number - 2, h + b, h), left
         else:
             src, dst, device = block(number - 5, b, h), block(number - 5, 0, h), right
+        arrival = halo_recv.at[stage, which if isinstance(which, int) else 0, number]
         return pltpu.make_async_remote_copy(
-            src_ref=src, dst_ref=dst,
-            send_sem=halo_send.at[stage, k, number], recv_sem=halo_recv.at[stage, k, number],
+            src_ref=src, dst_ref=dst, send_sem=halo_send.at[stage, number], recv_sem=arrival,
             device_id=device, device_id_type=MESH,
         )
 
@@ -260,24 +264,24 @@
         return y if x is None else jnp.logical_and(x, y)
 
     sends = [has_up, has_down] + [both(r, has_left) for r in rows_of] + [both(r, has_right) for r in rows_of]
-    sends = sends + sends[:2]
     gets = [has_down, has_up] + [both(r, has_right) for r in rows_of] + [both(r, has_left) for r in rows_of]
-    gets = gets + gets[:2]
-
-    def act(stage, k, number, what):
+
+    def act(stage, which, number, what, part=None):
         @pl.when(gets[number] if what == "wait_recv" else sends[number])
         def _():
-            getattr(halo(stage, k, number), what)()
+            getattr(halo(stage, which, number, part), what)()
 
     def begin_halo(stage, k, field, part):
         pads[stage, k, h + part * half : h + (part + 1) * half, h : h + b] = field
-        for number in (8 * part, 8 * part + 1) + ((3, 6) if part == 1 else ()):
-            act(stage, k, number, "start")
+        for number in (0, 1):
+            act(stage, k, number, "start", part)
+        if part == 1:
+            for number in (3, 6):
+                act(stage, k, number, "start")
 
     def forward(stage, k):
         for from_down, corners in ((0, (4, 7)), (1, (2, 5))):
-            for part in range(2):
-                act(stage, k, from_down + 8 * part, "wait_recv")
+            act(stage, k, from_down, "wait_recv")
             for number in corners:
                 act(stage, k, number, "start")
 
@@ -404,7 +408,7 @@
         label_col = jnp.sum(jnp.where(eye_slots, label, 0.0), axis=1, keepdims=True)
         chosen_keep[k] = (tile_lane == label_col).astype(jnp.bfloat16)
         swap_all(0, k).wait_recv()
-        head, rest = two_halves(flat(arrived, k))
+        head, rest = two_halves(flat(arrived[k]))
         totals = dot(
             jnp.concatenate([chosen_t, chosen_t], axis=1), jnp.concatenate([head, rest], axis=0)
         )
@@ -423,7 +427,10 @@
             begin_halo(1, k, jax.nn.sigmoid(heat), part)
         fill(1, k, 1, h, 0, b)
         own_rows(1, k, 0)
-    heat_done = pltpu.make_async_copy(heat_ref, heat_out, out_sems.at[here])
+    def stay(k):
+        return pltpu.make_async_copy(answers.at[k, me], returned.at[k, me], out_sems.at[2 + k])
+
+    heat_done = pltpu.make_async_copy(heat_ref, heat_out, out_sems.at[1])
     heat_done.start()
     run_stage(1)
     for k in range(here):
@@ -436,44 +443,50 @@
         for p in range(peers):
             answers[k, p] = answer[p * capacity : (p + 1) * capacity]
         start_each(functools.partial(swap_copy, 1, k))
-        returned[k, me] = answers[k, me]
+        stay(k).start()
     for stage in range(2):
+        for number in range(8):
+            act(stage, pl.ds(0, here), number, "wait_send")
         for k in range(here):
-            for number in range(10):
-                act(stage, k, number, "wait_send")
             for part in range(2):
                 share(stage, k, part).wait_send()
     label_all().wait_send()
     for k in range(here):
         swap_all(0, k).wait_send()
-    for k in range(here):
+    place_done.wait()
+    heat_done.wait()
+    for k in range(here):
+        stay(k).wait()
         swap_all(1, k).wait_recv()
-        head, rest = two_halves(flat(returned, k))
-        place = place_keep[k]
-        slopes_ref[k] = dot(
+    for k in range(here):
+        swap_all(1, k).wait_send()
+
+
+def finish_kernel(heat_in, returned, place_in, heat_out, slopes_out):
+    heat_out[...] = heat_in[...]
+    for k in range(place_in.shape[0]):
+        head, rest = two_halves(flat(returned[k]))
+        place = place_in[k]
+        slopes_out[k] = dot(
             jnp.concatenate([place, place], axis=1), jnp.concatenate([head, rest], axis=0)
         )
-        pltpu.make_async_copy(slopes_ref.at[k], slopes_out.at[k], out_sems.at[k]).start()
-    for k in range(here):
-        swap_all(1, k).wait_send()
-    heat_done.wait()
-    for k in range(here):
-        pltpu.make_async_copy(slopes_ref.at[k], slopes_out.at[k], out_sems.at[k]).wait()
-
-
-def finish_kernel(heat_in, slopes_in, heat_out, slopes_out):
-    heat_out[...] = heat_in[...]
-    slopes_out[...] = slopes_in[...]
-
-
-def finish(heat, slopes):
-    vmem = pl.BlockSpec(memory_space=pltpu.VMEM)
+
+
+def finish(heat, returned, place):
+    here, peers, capacity, cells = returned.shape
+    blocks, slots = place.shape[1:]
+    outs = (heat.shape, (here, blocks, cells))
+
+    def spec(shape):
+        return pl.BlockSpec((1, *shape[1:]), lambda k: (k,) + (0,) * (len(shape) - 1))
+
     return pl.pallas_call(
         finish_kernel,
-        out_shape=tuple(jax.ShapeDtypeStruct(x.shape, x.dtype) for x in (heat, slopes)),
-        in_specs=[vmem, vmem],
-        out_specs=(vmem, vmem),
-    )(heat, slopes)
+        grid=(here,),
+        out_shape=tuple(jax.ShapeDtypeStruct(x, jnp.float32) for x in outs),
+        in_specs=[spec(heat.shape), spec(returned.shape), spec(place.shape)],
+        out_specs=tuple(spec(x) for x in outs),
+    )(heat, returned, place)
 
 
 def local(parcel_patch, target_unit, target_patch, across_taps, down_taps, source_heated_mixing):
@@ -488,14 +501,15 @@
     f32, bf16 = jnp.float32, jnp.bfloat16
     swap_buffer = pltpu.VMEM((here, peers, capacity, cells), f32)
     sems = pltpu.SemaphoreType.DMA
-    heat, slopes = pl.pallas_call(
+    heat, returned, place = pl.pallas_call(
         kernel,
         out_shape=(
             jax.ShapeDtypeStruct((here, a, b), f32),
-            jax.ShapeDtypeStruct((here, blocks, cells), f32),
+            jax.ShapeDtypeStruct((here, peers, capacity, cells), f32),
+            jax.ShapeDtypeStruct((here, blocks, slots), bf16),
         ),
         in_specs=[anywhere] * 5 + [pl.BlockSpec(memory_space=pltpu.SMEM)],
-        out_specs=(anywhere, anywhere),
+        out_specs=(anywhere,) * 3,
         scratch_shapes=[
             pltpu.VMEM(parcel_patch.shape, f32),
             pltpu.VMEM((here, blocks), jnp.int32),
@@ -503,9 +517,8 @@
             pltpu.VMEM(across_taps.shape, f32),
             pltpu.VMEM(down_taps.shape, f32),
             pltpu.VMEM((here, a, b), f32),
-            pltpu.VMEM((here, blocks, cells), f32),
-            sems((5,)), sems((here + 1,)),
-            swap_buffer, swap_buffer, swap_buffer, swap_buffer,
+            sems((5,)), sems((here + 2,)),
+            swap_buffer, swap_buffer, swap_buffer,
             pltpu.VMEM((peers, 1, 128), f32),
             pltpu.VMEM((peers, 1, 128), f32),
             pltpu.VMEM((peers, 128), f32),
@@ -523,7 +536,7 @@
             pltpu.VMEM((2, dies, a, b), f32),
             pltpu.VMEM((2, here, a, b), f32),
             sems((2, here)), sems((2, here)), sems((2,)),
-            sems((2, here, 10)), sems((2, here, 10)),
+            sems((2, 8)), sems((2, here, 8)),
             sems((2, here, 2)), sems((2, here, 2)),
         ],
         compiler_params=pltpu.CompilerParams(
@@ -533,7 +546,7 @@
         parcel_patch, target_unit.reshape(here, blocks), target_patch,
         across_taps, down_taps, source_heated_mixing.transpose(1, 2, 0),
     )
-    return finish(heat, slopes)
+    return finish(heat, returned, place)
 
 
 def solution(mesh):

time: 73.7 us -> 72.9 us (0.989)
  Pallas kernels: 72.8 us -> 72 us
    pallas_call x1, Pallas kernels: 71 us -> 69.9 us  [local(): pl.pallas_call(kernel, out_shape=(jax.ShapeDtypeStruct((here, a, b), f32)...]
where the time goes in v4:
time: 72.9 us; the launch traced here: 72.7 us
  Pallas kernels  72 us (99%)
    pallas_call x1, Pallas kernels, local(): pl.pallas_call(kernel, out_shape=(jax.ShapeDtypeStruct((here, a, b), f32)...  69.9 us
    pallas_call x1, Pallas kernels, finish(): pl.pallas_call(finish_kernel, grid=(here,), out_shape=tuple((jax.ShapeDty...  2.08 us

profile of v4, /device:TPU:0, one launch (start us, length us, event | category | flops | bytes accessed | tf_op | source)
XLA Modules:
  0.0 72.7 jit_solution(13767550183255692315)
XLA Ops:
  0.6 69.9 %shard_map.77 = (f32[2,128,256]{2,1,0:T(8,128)}, f32[2,16,16,256]{3,2,1,0:T(8,128)}, bf16[2,128,256]{2,1,0:T(8,128)(2,1)}) custom-call(f32[2,128,256]{2,1,0:T(8,128)} %patch_in.1, s32[2,128]{1,0:T(2,128)} %bitcast.3, s32[2,128]{1,0:T(2,128)} %tile_in.1, f32[8,255]{1,0:T(8,128)} %across_in.1, f32[8,255]{1,0:T(8,128)} %down_in.1, f32[4,4,8]{2,1,0:T(4,128)} %bitcast.2), custom_call_target="tpu_custom_call" | custom-call | tf_op jit(solution)/shard_map/pallas_call | solution.py:504
  70.6 2.1 %shard_map.78 = (f32[2,128,256]{2,1,0:T(8,128)}, f32[2,128,256]{2,1,0:T(8,128)}) custom-call(f32[2,128,256]{2,1,0:T(8,128)} %get-tuple-element.5.heat_in, f32[2,16,16,256]{3,2,1,0:T(8,128)} %get-tuple-element.6.returned, bf16[2,128,256]{2,1,0:T(8,128)(2,1)} %get-tuple-element.7.place_in), custom_call_target="tpu_custom_call" | custom-call | tf_op jit(solution)/shard_map/pallas_call | solution.py:483

commit v5 on v4

--- a/solution.py
+++ b/solution.py
@@ -168,7 +168,7 @@
 
     def start_each(make):
         def body(j, carry):
-            make((j + peers // 2 - 2) % (peers - 1) + 1).start()
+            make(j).start()
             return carry
 
         lax.fori_loop(1, peers, body, 0)

time: 72.9 us -> 69 us (0.947)
  Pallas kernels: 72 us -> 68.1 us
    pallas_call x1, Pallas kernels: 69.9 us -> 66.1 us  [local(): pl.pallas_call(kernel, out_shape=(jax.ShapeDtypeStruct((here, a, b), f32)...]
where the time goes in v5:
time: 69 us; the launch traced here: 68.8 us
  Pallas kernels  68.1 us (99%)
    pallas_call x1, Pallas kernels, local(): pl.pallas_call(kernel, out_shape=(jax.ShapeDtypeStruct((here, a, b), f32)...  66.1 us
    pallas_call x1, Pallas kernels, finish(): pl.pallas_call(finish_kernel, grid=(here,), out_shape=tuple((jax.ShapeDty...  2.08 us

profile of v5, /device:TPU:0, one launch (start us, length us, event | category | flops | bytes accessed | tf_op | source)
XLA Modules:
  0.0 68.8 jit_solution(5712844426865581692)
XLA Ops:
  0.6 66.1 %shard_map.77 = (f32[2,128,256]{2,1,0:T(8,128)}, f32[2,16,16,256]{3,2,1,0:T(8,128)}, bf16[2,128,256]{2,1,0:T(8,128)(2,1)}) custom-call(f32[2,128,256]{2,1,0:T(8,128)} %patch_in.1, s32[2,128]{1,0:T(2,128)} %bitcast.3, s32[2,128]{1,0:T(2,128)} %tile_in.1, f32[8,255]{1,0:T(8,128)} %across_in.1, f32[8,255]{1,0:T(8,128)} %down_in.1, f32[4,4,8]{2,1,0:T(4,128)} %bitcast.2), custom_call_target="tpu_custom_call" | custom-call | tf_op jit(solution)/shard_map/pallas_call | solution.py:504
  66.7 2.1 %shard_map.78 = (f32[2,128,256]{2,1,0:T(8,128)}, f32[2,128,256]{2,1,0:T(8,128)}) custom-call(f32[2,128,256]{2,1,0:T(8,128)} %get-tuple-element.5.heat_in, f32[2,16,16,256]{3,2,1,0:T(8,128)} %get-tuple-element.6.returned, bf16[2,128,256]{2,1,0:T(8,128)(2,1)} %get-tuple-element.7.place_in), custom_call_target="tpu_custom_call" | custom-call | tf_op jit(solution)/shard_map/pallas_call | solution.py:483

commit v6 on v5

--- a/solution.py
+++ b/solution.py
@@ -273,8 +273,9 @@
 
     def begin_halo(stage, k, field, part):
         pads[stage, k, h + part * half : h + (part + 1) * half, h : h + b] = field
-        for number in (0, 1):
-            act(stage, k, number, "start", part)
+        if stage == 1 or part == 1:
+            for number in (0, 1):
+                act(stage, k, number, "start", part if stage == 1 else None)
         if part == 1:
             for number in (3, 6):
                 act(stage, k, number, "start")

time: 69 us -> 69 us (level)
  no operation moved by 1% of the time
where the time goes in v6:
time: 69 us; the launch traced here: 68.8 us
  Pallas kernels  68.2 us (99%)
    pallas_call x1, Pallas kernels, local(): pl.pallas_call(kernel, out_shape=(jax.ShapeDtypeStruct((here, a, b), f32)...  66.1 us
    pallas_call x1, Pallas kernels, finish(): pl.pallas_call(finish_kernel, grid=(here,), out_shape=tuple((jax.ShapeDty...  2.08 us

profile of v6, /device:TPU:0, one launch (start us, length us, event | category | flops | bytes accessed | tf_op | source)
XLA Modules:
  0.0 68.8 jit_solution(4391641913828915126)
XLA Ops:
  0.6 66.1 %shard_map.77 = (f32[2,128,256]{2,1,0:T(8,128)}, f32[2,16,16,256]{3,2,1,0:T(8,128)}, bf16[2,128,256]{2,1,0:T(8,128)(2,1)}) custom-call(f32[2,128,256]{2,1,0:T(8,128)} %patch_in.1, s32[2,128]{1,0:T(2,128)} %bitcast.3, s32[2,128]{1,0:T(2,128)} %tile_in.1, f32[8,255]{1,0:T(8,128)} %across_in.1, f32[8,255]{1,0:T(8,128)} %down_in.1, f32[4,4,8]{2,1,0:T(4,128)} %bitcast.2), custom_call_target="tpu_custom_call" | custom-call | tf_op jit(solution)/shard_map/pallas_call | solution.py:505
  66.7 2.1 %shard_map.78 = (f32[2,128,256]{2,1,0:T(8,128)}, f32[2,128,256]{2,1,0:T(8,128)}) custom-call(f32[2,128,256]{2,1,0:T(8,128)} %get-tuple-element.5.heat_in, f32[2,16,16,256]{3,2,1,0:T(8,128)} %get-tuple-element.6.returned, bf16[2,128,256]{2,1,0:T(8,128)(2,1)} %get-tuple-element.7.place_in), custom_call_target="tpu_custom_call" | custom-call | tf_op jit(solution)/shard_map/pallas_call | solution.py:484
